TPU v7x, 32 devices: a whole 2x2x4 slice. The times are simulated.
32 devices in a mesh: head: 8 (over z, core), seq: 4 (over y, x).
Axes of the slice: x: 2, y: 2, z: 4, core: 2. Of those that a mesh axis runs over, the one named last changes fastest.
Arguments:
- queries: bfloat16 [8, 8192, 64], P('head', 'seq'), may hold values from -160 to 160
- keys: bfloat16 [8, 8192, 64], P('head', 'seq'), may hold values from -8 to 8
- values: bfloat16 [8, 8192, 64], P('head', 'seq'), may hold values from -20 to 20
- block_mask: int32 [8, 16, 64], P('head'), may hold values from 0 to 1, as said below
- block_order: int32 [16], replicated, may hold values from 0 to 15, as said below
- sparse_gain: float32 [8, 64], P('head'), may hold values from 0.1 to 1.9
- linear_gain: float32 [8, 64], P('head'), may hold values from 0.1 to 1.9
Outputs:
- mixed: float32 [8, 8192, 64], P('head', 'seq')
Inputs may be any that keep to these rules, and one draw needn't show every extreme that they name: A permutation of the query blocks; rows b * 512 to (b + 1) * 512 - 1 of queries and mixed belong to query block block_order[b]. Each row block_mask[h, n] has exactly 6 ones; at most 2 of them lie among the 16 key blocks of one index of seq, and in every row some index holds exactly 2; key block n * 4 is always selected by query block n.
All inputs are finite; a program needn't handle non-finite values.
Results may differ from a plain program's by a relative error of at most 0.002.
Values may be sent and summed in bfloat16 or wider, within the bound.
A program may use at most 64 MiB of HBM per device.

v0:
```python
import jax
import jax.numpy as jnp
from jax import lax
from jax.sharding import PartitionSpec as P

BQ = 512
BK = 128


EPSILON = 1e-06
TOP_PRECISION = lax.Precision.HIGHEST
TRIPLE_PASS_MODE = lax.Precision.HIGH
NEGATIVE = -1e30


def feature(values_in):
    return jax.nn.elu(values_in) + 1.0


def body(queries, keys, values, block_mask, block_order, sparse_gain, linear_gain):
    tokens_dev = queries.shape[1]
    head_width = queries.shape[2]
    seq_count = lax.axis_size("seq")
    seq_index = lax.axis_index("seq")
    query_count = tokens_dev // BQ
    key_count = tokens_dev // BK
    block_total = key_count * seq_count
    chosen_count = block_total // 10
    slot_count = max(2, chosen_count // seq_count + 1)
    score_scale = head_width ** (-0.5)
    positions = block_order.shape[0]
    order_hot = (block_order[:, None] == jnp.arange(positions, dtype=jnp.int32)[None, :]).astype(
        jnp.float32
    )
    ordered_mask = jnp.dot(order_hot, block_mask[0].astype(jnp.float32), precision=TOP_PRECISION)
    own_rows = lax.dynamic_slice_in_dim(ordered_mask, seq_index * query_count, query_count, 0)
    local_cols = lax.dynamic_slice_in_dim(ordered_mask, seq_index * key_count, key_count, 1)
    query_blocks = queries[0].reshape(query_count, BQ, head_width)
    key_local = keys[0]
    value_local = values[0]
    feat_keys = feature(key_local.astype(jnp.float32)).reshape(key_count, BK, head_width)
    value_float = value_local.astype(jnp.float32).reshape(key_count, BK, head_width)
    states = jnp.einsum("jtd,jte->jde", feat_keys, value_float, precision=TRIPLE_PASS_MODE).reshape(
        key_count, head_width * head_width
    )
    key_sums = jnp.sum(feat_keys, axis=1)
    paired = jnp.concatenate([key_local, value_local], axis=1)

    def attend(block_item):
        query_block, pair_block, live_keys = block_item
        keys_block = pair_block[:, :head_width]
        values_block = pair_block[:, head_width:]
        tile_relevance = (
            jnp.einsum("qd,kd->qk", query_block, keys_block, preferred_element_type=jnp.float32)
            * score_scale
        )
        alive = live_keys[None, :] > 0.5
        tile_relevance = jnp.where(alive, tile_relevance, NEGATIVE)
        row_top = jnp.max(tile_relevance, axis=1, keepdims=True)
        weights = jnp.where(alive, jnp.exp(tile_relevance - row_top), 0.0)
        row_total = jnp.sum(weights, axis=1, keepdims=True)
        output = (
            jnp.dot(weights.astype(jnp.bfloat16), values_block, preferred_element_type=jnp.float32)
            / row_total
        )
        chosen_state = jnp.zeros((head_width * head_width,), jnp.float32)
        chosen_sum = jnp.zeros((head_width,), jnp.float32)
        return (output, chosen_state, chosen_sum)

    tile_ordinals = jnp.cumsum(local_cols, axis=1) - 1.0
    slot_ids = jnp.arange(slot_count, dtype=jnp.float32)
    picker = local_cols[:, None, :] * (tile_ordinals[:, None, :] == slot_ids[None, :, None]).astype(
        jnp.float32
    )
    flat_pairs = paired.reshape(key_count, BK * 2 * head_width)
    outgoing = jnp.dot(
        picker.reshape(positions * slot_count, key_count).astype(jnp.bfloat16),
        flat_pairs,
        preferred_element_type=jnp.float32,
    ).astype(jnp.bfloat16)
    outgoing = outgoing.reshape(seq_count, query_count, slot_count * BK, 2 * head_width)
    incoming = lax.all_to_all(outgoing, "seq", split_axis=0, concat_axis=2, tiled=True)
    pair_blocks = incoming.reshape(query_count, seq_count * slot_count * BK, 2 * head_width)
    counts = jnp.sum(own_rows.reshape(query_count, seq_count, key_count), axis=2)
    live = (slot_ids[None, None, :] < counts[:, :, None]).astype(jnp.float32)
    live_keys = jnp.broadcast_to(
        live[:, :, :, None], (query_count, seq_count, slot_count, BK)
    ).reshape(query_count, seq_count * slot_count * BK)
    sparse_blocks, chosen_states, chosen_sums = lax.map(
        attend, (query_blocks, pair_blocks, live_keys)
    )
    sparse = sparse_blocks.reshape(tokens_dev, head_width)
    all_states, all_sums = (
        lax.all_gather(states, "seq", axis=0, tiled=True),
        lax.all_gather(key_sums, "seq", axis=0, tiled=True),
    )
    unselected = 1.0 - own_rows
    remaining_states = jnp.dot(unselected, all_states, precision=TOP_PRECISION)
    remaining_sums = jnp.dot(unselected, all_sums, precision=TOP_PRECISION)
    feature_query = feature(query_blocks.astype(jnp.float32))
    numerator = jnp.einsum(
        "svo,sol->svl",
        feature_query,
        remaining_states.reshape(query_count, head_width, head_width),
        precision=TRIPLE_PASS_MODE,
    )
    denominator = jnp.einsum(
        "ryh,rh->ry", feature_query, remaining_sums, precision=TRIPLE_PASS_MODE
    )
    linear = (numerator / denominator[:, :, None]).reshape(tokens_dev, head_width)
    square_sparse = jnp.sum(sparse * sparse, axis=1)
    square_linear = jnp.sum(linear * linear, axis=1)
    total_sparse, total_linear = lax.psum((square_sparse, square_linear), "head")
    features = lax.axis_size("head") * queries.shape[0] * head_width
    rms_sparse = jnp.sqrt(total_sparse / features + EPSILON)
    rms_linear = jnp.sqrt(total_linear / features + EPSILON)
    first = sparse / rms_sparse[:, None] * sparse_gain[0][None, :]
    second = linear / rms_linear[:, None] * linear_gain[0][None, :]
    return (first + second)[None]


def solution(mesh):
    in_specs = (
        P("head", "seq", None),
        P("head", "seq", None),
        P("head", "seq", None),
        P("head", None, None),
        P(),
        P("head", None),
        P("head", None),
    )
    out_specs = P("head", "seq", None)
    return jax.shard_map(body, mesh=mesh, in_specs=in_specs, out_specs=out_specs, check_vma=False)
```

profile of v0, /device:TPU:0, one launch (start us, length us, event | category | flops | bytes accessed | tf_op | source)
XLA Modules:
  0.0 87.6 jit_solution(2472979980419307682)
XLA Ops:
  6.5 0.9 %fusion.37 = f32[16,64]{1,0:T(8,128)S(1)} fusion(s32[1,16,64]{2,1,0:T(8,128)} %param.12, s32[16]{0:T(128)} %param.13), kind=kOutput, calls=%fused_computation.50 | convolution fusion | flops 197888 | bytes 8256 | tf_op jit(solution)/shard_map/dot_general | solution.py:35
  7.7 1.1 %pad_maximum_fusion = bf16[2048,128]{0,1:T(8,128)(2,1)S(1)} fusion(bf16[2048,64]{0,1:T(8,128)(2,1)} %bitcast.68, bf16[2048,64]{0,1:T(8,128)(2,1)} %bitcast.67), kind=kLoop, calls=%fused_computation.34 | loop fusion | flops 1048576 | bytes 1048576 | tf_op jit(solution)/shard_map/concatenate | solution.py:47
  9.7 1.3 %reshape.209 = bf16[4,4,256,128]{3,2,1,0:T(8,128)(2,1)} reshape(bf16[32,16384]{1,0:T(8,128)(2,1)S(1)} %convolution_convert_fusion) | data formatting | bytes 2097152 | tf_op jit(solution)/shard_map/reshape | solution.py:81
  11.1 5.3 %all-to-all-start = ((bf16[4,4,256,128]{3,2,1,0:T(8,128)(2,1)}), bf16[4,4,256,128]{3,2,1,0:T(8,128)(2,1)S(1)}, u32[]{:S(2)}, u32[]{:S(2)}) async-start(bf16[4,4,256,128]{3,2,1,0:T(8,128)(2,1)} %reshape.209), calls=%async_computation | async-start | bytes 2097152 | tf_op jit(solution)/shard_map/all_to_all | solution.py:82
  16.6 0.6 fusion.31
  17.2 0.9 %reshape.213 = f32[16,4096]{1,0:T(8,128)} reshape(f32[16,64,64]{2,1,0:T(8,128)S(1)} %fusion.31) | data formatting | bytes 524288 | tf_op jit(solution)/shard_map/reshape | solution.py:43
  19.1 14.3 %all_gather.7 = f32[64,64]{1,0:T(8,128)S(1)} all-gather(f32[16,64]{1,0:T(8,128)S(1)} %fusion.30), channel_id=1, replica_groups=mesh['head'=8,'seq'=4] {'seq'}, dimensions={0}, use_global_device_ids=true | all-gather | bytes 20480 | tf_op jit(solution)/shard_map/all_gather | solution.py:95
  33.5 0.9 %fusion.21 = f32[4,1,512]{2,1,0:T(1,128)S(1)} fusion(f32[4,64,1]{1,2,0:T(1,128)S(1)} %bitcast.77, bf16[4,512,64]{2,1,0:T(8,128)(2,1)S(1)} %bitcast.63), kind=kOutput, calls=%fused_computation.31 | convolution fusion | flops 1441792 | bytes 271360 | tf_op jit(solution)/shard_map/ryh,rh->ry/dot_general | solution.py:107
  34.6 7.7 %while.10 = (s32[]{:T(128)}, f32[4,512,64]{1,2,0:T(8,128)S(1)}, f32[4,1024]{1,0:T(4,128)S(1)}, bf16[4,512,64]{2,1,0:T(8,128)(2,1)S(1)}, bf16[4,1024,128]{2,1,0:T(8,128)(2,1)S(1)}, /*index=5*/s32[]{:T(128)}) while((s32[]{:T(128)}, f32[4,512,64]{1,2,0:T(8,128)S(1)}, f32[4,1024]{1,0:T(4,128)S(1)}, bf16[4,512,64]{2,1,0:T(8,128)(2,1)S(1)}, ...), condition=%wide.region_5.6_spmd, body=%wide.region_2.5_spmd.sunk | while | flops 141066240 | bytes 7620693 | solution.py:89
  34.7 0.5 fusion.69
  35.2 0.6 fusion.70
  35.9 0.7 fusion.71
  36.6 0.5 fusion.69
  37.1 0.6 fusion.70
  37.8 0.7 fusion.71
  39.1 0.6 fusion.70
  39.7 0.7 fusion.71
  41.0 0.6 fusion.70
  41.6 0.7 fusion.71
  43.1 4.4 %all-gather.2.cloned.1.call-done = f32[64,4096]{1,0:T(8,128)} async-done(((f32[16,4096]{1,0:T(8,128)}), f32[64,4096]{1,0:T(8,128)}) %all-gather.2.cloned.1.call-update) | async-done | bytes 1048592 | tf_op jit(solution)/shard_map/all_gather | solution.py:94
  47.6 1.8 %fusion.44 = f32[4,4096]{1,0:T(4,128)S(1)} fusion(f32[64,4096]{1,0:T(8,128)} %all-gather.2.cloned.1.call-done, f32[4,64]{1,0:T(4,128)S(1)} %constant_dynamic-slice_fusion.1), kind=kOutput, calls=%fused_computation.63 | convolution fusion | flops 12583168 | bytes 1115136 | tf_op jit(solution)/shard_map/dot_general | solution.py:98
  49.5 1.1 %multiply_reduce_fusion = (f32[4,512]{1,0:T(4,128)S(1)}, f32[4,512,64]{1,2,0:T(8,128)S(1)}) fusion(f32[4,512]{1,0:T(4,128)S(1)} %bitcast.75, f32[4,64,64]{2,1,0:T(8,128)S(1)} %reshape.214, bf16[4,512,64]{2,1,0:T(8,128)(2,1)S(1)} %get-tuple-element.106), kind=kOutput, calls=%fused_computation.39 | convolution fusion | flops 51378176 | bytes 868352 | tf_op jit(solution)/shard_map/svo,sol->svl/dot_general | solution.py:101
  51.4 28.5 %all-reduce = (f32[2048]{0:T(1024)S(1)}, f32[2048]{0:T(1024)S(1)}) all-reduce(f32[2048]{0:T(1024)S(1)} %bitcast.74, f32[2048]{0:T(1024)S(1)} %bitcast.73), channel_id=1, replica_groups=mesh['head'=8,'seq'=4] {'head'}, use_global_device_ids=true, to_apply=%region_10.11 | all-reduce | flops 4096 | bytes 32768 | tf_op jit(solution)/shard_map/psum | solution.py:113
  79.9 0.9 %multiply_add_fusion = f32[1,2048,64]{1,2,0:T(8,128)} fusion(f32[1,2048,64]{1,2,0:T(8,128)S(1)} %reshape.215, f32[1,2048,64]{1,2,0:T(8,128)S(1)} %reshape.211, f32[64]{0:T(128)S(1)} %bitcast.78, f32[2048]{0:T(1024)S(1)} %get-tuple-element.49, f32[64]{0:T(128)S(1)} %bitcast.79, f32[2048]{0:T(1024)S(1)} %get-tuple-element.50), kind=kLoop, calls=%fused_computation.38 | loop fusion | flops 655360 | bytes 1589760 | tf_op jit(solution)/shard_map/add | solution.py:119
  (54 shorter events, 5.5 us)
Async XLA Ops:
  9.7 6.6 %copy-start = (bf16[1,2048,64]{1,2,0:T(8,128)(2,1)S(1)}, bf16[1,2048,64]{1,2,0:T(8,128)(2,1)}, u32[]{:S(2)}) copy-start(bf16[1,2048,64]{1,2,0:T(8,128)(2,1)} %param.10) | copy-start | bytes 786436
  11.0 5.5 %copy-start.1 = (bf16[1,2048,64]{1,2,0:T(8,128)(2,1)S(1)}, bf16[1,2048,64]{1,2,0:T(8,128)(2,1)}, u32[]{:S(2)}) copy-start(bf16[1,2048,64]{1,2,0:T(8,128)(2,1)} %param.11) | copy-start | bytes 786436
  11.1 23.5 %all-to-all-start = ((bf16[4,4,256,128]{3,2,1,0:T(8,128)(2,1)}), bf16[4,4,256,128]{3,2,1,0:T(8,128)(2,1)S(1)}, u32[]{:S(2)}, u32[]{:S(2)}) async-start(bf16[4,4,256,128]{3,2,1,0:T(8,128)(2,1)} %reshape.209), calls=%async_computation | async-start | bytes 2097152 | tf_op jit(solution)/shard_map/all_to_all | solution.py:82
  16.3 31.2 %all-gather.2.cloned.1.call-start = ((), (), s32[]{:S(2)}) async-start(), calls=%async_computation.1 | async-start | bytes 1310720 | tf_op jit(solution)/shard_map/all_gather | solution.py:94
  16.4 2.1 %copy-start.2 = (bf16[1,2048,64]{1,2,0:T(8,128)(2,1)S(1)}, bf16[1,2048,64]{1,2,0:T(8,128)(2,1)}, u32[]{:S(2)}) copy-start(bf16[1,2048,64]{1,2,0:T(8,128)(2,1)} %param.9) | copy-start | bytes 786436
  50.6 29.2 %copy-start.3 = (f32[1,64]{1,0:T(1,128)S(1)}, f32[1,64]{1,0:T(1,128)}, u32[]{:S(2)}) copy-start(f32[1,64]{1,0:T(1,128)} %param.15) | copy-start | bytes 772
  50.6 29.2 %copy-start.4 = (f32[1,64]{1,0:T(1,128)S(1)}, f32[1,64]{1,0:T(1,128)}, u32[]{:S(2)}) copy-start(f32[1,64]{1,0:T(1,128)} %param.14) | copy-start | bytes 772
Sparse Core Ops, SparseCore 0:
  19.0 28.5 all-gather.1
where the time goes:
time: 88 us; the launch traced here: 87.6 us
  blocking collectives  42.7 us (49%)
  between operations  13.6 us (15%)
  matrix products  10.7 us (12%)
  other arithmetic  5.54 us (6%)
  starting transfers between devices  5.3 us (6%)
  local copies, waits for them, and re-layouts  5.17 us (6%)
  waiting for transfers between devices  4.46 us (5%)
    psum x1, blocking collectives, body(): lax.psum((square_sparse, square_linear), 'head')  28.5 us
    all_gather x1, blocking collectives, body(): lax.all_gather(key_sums, 'seq', axis=0, tiled=True)  14.3 us
    all_to_all x1, starting transfers between devices, body(): lax.all_to_all(outgoing, 'seq', split_axis=0, concat_axis=2, tiled=True)  5.3 us
    all_gather x1, waiting for transfers between devices, body(): lax.all_gather(states, 'seq', axis=0, tiled=True)  4.43 us
    dot_general x4, matrix products, attend(): jnp.dot(weights.astype(jnp.bfloat16), values_block, preferred_element_typ...  2.69 us
    reduce_sum x4, other arithmetic, attend(): row_total = jnp.sum(weights, axis=1, keepdims=True)  2.58 us
    dot_general x4, matrix products, attend(): jnp.einsum('qd,kd->qk', query_block, keys_block, preferred_element_type=j...  2.1 us
    dot_general x1, matrix products, body(): remaining_states = jnp.dot(unselected, all_states, precision=TOP_PRECISION)  1.83 us
  transfers between devices with their start and end apart: 2, of which 1 were waited for; matrix products, arithmetic and copies ran while one was open for 14% of the time, Pallas kernels for 0%

commit v1 on v0

v1 whole, which is shorter than its diff:
```python
import functools

import jax
import jax.numpy as jnp
from jax import lax
from jax.experimental import pallas as pl
from jax.experimental.pallas import tpu as pltpu
from jax.sharding import PartitionSpec as P

BQ = 512
BK = 128
SLOTS = 2
EPSILON = 1e-06
NEGATIVE = -1e30
MESH = pl.DeviceIdType.MESH


def phi(x):
    return jnp.where(x > 0, x + 1.0, jnp.exp(jnp.minimum(x, 0.0)))


def pack(pick_ref, k_ref, v_ref, out_ref):
    n_seq, n_query = out_ref.shape[:2]

    @pl.loop(0, n_seq)
    def _(dev):
        for b in range(n_query):
            for s in range(SLOTS):
                block = pick_ref[(dev * n_query + b) * SLOTS + s]
                columns = pl.ds(pl.multiple_of(block * BK, BK), BK)
                out_ref[dev, b, 0, :, s * BK : (s + 1) * BK] = k_ref[:, columns]
                out_ref[dev, b, 1, :, s * BK : (s + 1) * BK] = v_ref[:, columns]


def kernel(
    n_seq, n_head, n_query, n_key, features,
    bias_ref, send, q_ref, k_ref, v_ref, coef_ref, gain_ref, out_ref,
    recv, usend, urecv, states, scores, sq, linear_ref, sparse_ref,
    kv_send_sem, kv_recv_sem, u_send_sem, u_recv_sem, sq_send_sem, sq_recv_sem,
):
    me = lax.axis_index("seq")
    head = lax.axis_index("head")
    width = q_ref.shape[0]
    rows = usend.shape[2]
    pairs = n_query // 2

    def peer(o):
        return lax.rem(me + o, n_seq)

    def head_peer(o):
        return lax.rem(head + o, n_head)

    def kv_copy(dev, at, b):
        return pltpu.make_async_remote_copy(
            src_ref=send.at[dev, b], dst_ref=recv.at[at, b],
            send_sem=kv_send_sem.at[dev, b], recv_sem=kv_recv_sem.at[at, b],
            device_id={"seq": dev}, device_id_type=MESH,
        )

    def u_copy(dev, at):
        return pltpu.make_async_remote_copy(
            src_ref=usend.at[dev], dst_ref=urecv.at[at],
            send_sem=u_send_sem.at[dev], recv_sem=u_recv_sem.at[at],
            device_id={"seq": dev}, device_id_type=MESH,
        )

    def sq_copy(dev, at, b):
        return pltpu.make_async_remote_copy(
            src_ref=sq.at[head, b], dst_ref=sq.at[at, b],
            send_sem=sq_send_sem.at[dev, b], recv_sem=sq_recv_sem.at[at, b],
            device_id={"head": dev}, device_id_type=MESH,
        )

    barrier = pltpu.get_barrier_semaphore()

    @pl.loop(1, n_seq)
    def _(o):
        pl.semaphore_signal(barrier, inc=1, device_id={"seq": peer(o)}, device_id_type=MESH)

    @pl.loop(1, n_head)
    def _(o):
        pl.semaphore_signal(barrier, inc=1, device_id={"head": head_peer(o)}, device_id_type=MESH)

    pl.semaphore_wait(barrier, n_seq + n_head - 2)
    for b in range(n_query):

        @pl.loop(1, n_seq)
        def _(o):
            kv_copy(peer(o), me, b).start()

    ones = jnp.ones((16, BK), jnp.bfloat16)
    for j in range(n_key):
        columns = slice(j * BK, (j + 1) * BK)
        feat = phi(k_ref[:, columns].astype(jnp.float32))
        feat = jnp.concatenate([feat, feat], axis=0)
        high = feat.astype(jnp.bfloat16)
        low = (feat - high.astype(jnp.float32)).astype(jnp.bfloat16)
        wide = jnp.concatenate([v_ref[:, columns], ones], axis=0)
        dims = (((1,), (1,)), ((), ()))
        state = lax.dot_general(wide, high, dims, preferred_element_type=jnp.float32)
        state += lax.dot_general(wide, low, dims, preferred_element_type=jnp.float32)
        states[j] = state[:rows]

    def combine(dev, target, place):
        for p in range(pairs):
            total = jnp.zeros((rows, 2 * width), jnp.float32)
            for j in range(n_key):
                total += states[j] * coef_ref[dev * pairs + p, j : j + 1, :]
            target[place, p] = total

    @pl.loop(1, n_seq)
    def _(o):
        combine(peer(o), usend, peer(o))
        u_copy(peer(o), me).start()

    combine(me, urecv, me)
    recv[me] = send[me]

    @pl.loop(1, n_seq)
    def _(o):
        u_copy(peer(o), peer(o)).wait_recv()

    def sums(x):
        total = jnp.sum(x * x, axis=0, keepdims=True)
        return [total[:, i * BK : (i + 1) * BK] for i in range(BQ // BK)]

    @pl.loop(0, pairs)
    def _(p):
        state = urecv[0, p]
        for src in range(1, n_seq):
            state += urecv[src, p]
        for half in range(2):
            b = p * 2 + half
            here = pl.ds(pl.multiple_of(b * BQ, BQ), BQ)
            query = q_ref[:, here].astype(jnp.float32)
            mine = jnp.dot(
                state[:, half * width : (half + 1) * width], phi(query),
                preferred_element_type=jnp.float32, precision=lax.Precision.HIGH,
            )
            linear = mine[:width] / mine[width : width + 1]
            linear_ref[:, here] = linear
            scaled = (query * width ** (-0.5)).astype(jnp.bfloat16)

            @pl.loop(1, n_seq)
            def _(o):
                kv_copy(peer(o), peer(o), b).wait_recv()

            top = jnp.full((1, BQ), NEGATIVE, jnp.float32)
            for src in range(n_seq):
                part = lax.dot_general(
                    recv[src, b, 0], scaled, (((0,), (0,)), ((), ())),
                    preferred_element_type=jnp.float32,
                )
                for s in range(SLOTS):
                    one = part[s * BK : (s + 1) * BK] + bias_ref[(b * n_seq + src) * SLOTS + s]
                    scores[src, s * BK : (s + 1) * BK] = one
                    top = jnp.maximum(top, jnp.max(one, axis=0, keepdims=True))
            total = jnp.zeros((1, BQ), jnp.float32)
            acc = jnp.zeros((width, BQ), jnp.float32)
            for src in range(n_seq):
                weights = jnp.exp(scores[src] - top)
                total += jnp.sum(weights, axis=0, keepdims=True)
                acc += jnp.dot(
                    recv[src, b, 1], weights.astype(jnp.bfloat16),
                    preferred_element_type=jnp.float32,
                )
            sparse = acc / total
            sparse_ref[:, here] = sparse
            sq[head, b] = jnp.concatenate(sums(sparse) + sums(linear), axis=0)

            @pl.loop(1, n_head)
            def _(o):
                sq_copy(head_peer(o), head, b).start()

    gain_sparse = gain_ref[:, 0:1]
    gain_linear = gain_ref[:, 1:2]

    @pl.loop(0, n_query)
    def _(b):
        @pl.loop(1, n_head)
        def _(o):
            sq_copy(head_peer(o), head_peer(o), b).wait_recv()

        total = sq[0, b]
        for h in range(1, n_head):
            total += sq[h, b]
        scale = 1.0 / jnp.sqrt(total / features + EPSILON)
        parts = BQ // BK
        for i in range(parts):
            here = pl.ds(pl.multiple_of(b * BQ + i * BK, BK), BK)
            first = sparse_ref[:, here] * scale[i : i + 1] * gain_sparse
            second = linear_ref[:, here] * scale[parts + i : parts + i + 1] * gain_linear
            out_ref[:, here] = first + second

    @pl.loop(1, n_seq)
    def _(o):
        u_copy(peer(o), me).wait_send()
        for b in range(n_query):
            kv_copy(peer(o), me, b).wait_send()

    @pl.loop(1, n_head)
    def _(o):
        for b in range(n_query):
            sq_copy(head_peer(o), head, b).wait_send()


def body(queries, keys, values, block_mask, block_order, sparse_gain, linear_gain):
    tokens, width = queries.shape[1:]
    n_seq, n_head = lax.axis_size("seq"), lax.axis_size("head")
    me = lax.axis_index("seq")
    n_query, n_key = tokens // BQ, tokens // BK
    positions = block_order.shape[0]
    pairs = n_query // 2
    hot = block_order[:, None] == jnp.arange(positions, dtype=jnp.int32)[None, :]
    ordered = jnp.sum(jnp.where(hot[:, :, None], block_mask[0][None], 0), axis=1)
    local = lax.dynamic_slice_in_dim(ordered, me * n_key, n_key, 1)
    own = lax.dynamic_slice_in_dim(ordered, me * n_query, n_query, 0)
    column = jnp.arange(n_key, dtype=jnp.int32)[None, :]
    first = jnp.min(jnp.where(local > 0, column, n_key), axis=1)
    last = jnp.max(jnp.where(local > 0, column, 0), axis=1)
    pick = jnp.stack([jnp.minimum(first, n_key - 1), last], axis=1).reshape(-1)
    count = jnp.sum(own.reshape(n_query, n_seq, n_key), axis=2)
    slot = jnp.arange(SLOTS, dtype=jnp.int32)
    bias = jnp.where(slot < count[:, :, None], 0.0, NEGATIVE).astype(jnp.float32).reshape(-1)
    open_blocks = 1.0 - local.astype(jnp.float32)
    coef = open_blocks.reshape(n_seq * pairs, 2, n_key).swapaxes(1, 2)
    coef = jnp.repeat(coef, width, axis=2)
    gains = jnp.concatenate([sparse_gain, linear_gain], axis=0).T
    rows = width + 8
    vmem = pl.BlockSpec(memory_space=pltpu.VMEM)
    smem = pl.BlockSpec(memory_space=pltpu.SMEM)
    dma = pltpu.SemaphoreType.DMA
    packed = pl.pallas_call(
        pack,
        out_shape=jax.ShapeDtypeStruct(
            (n_seq, n_query, 2, width, SLOTS * BK), jnp.bfloat16
        ),
        in_specs=[smem, vmem, vmem],
        out_specs=vmem,
        compiler_params=pltpu.CompilerParams(vmem_limit_bytes=24 * 1024 * 1024),
    )(pick, keys[0].T, values[0].T)
    out = pl.pallas_call(
        functools.partial(
            kernel, n_seq, n_head, n_query, n_key, n_head * queries.shape[0] * width
        ),
        out_shape=jax.ShapeDtypeStruct((width, tokens), jnp.float32),
        in_specs=[smem] + [vmem] * 6,
        out_specs=vmem,
        scratch_shapes=[
            pltpu.VMEM((n_seq, n_query, 2, width, SLOTS * BK), jnp.bfloat16),
            pltpu.VMEM((n_seq, pairs, rows, 2 * width), jnp.float32),
            pltpu.VMEM((n_seq, pairs, rows, 2 * width), jnp.float32),
            pltpu.VMEM((n_key, rows, 2 * width), jnp.float32),
            pltpu.VMEM((n_seq, SLOTS * BK, BQ), jnp.float32),
            pltpu.VMEM((n_head, n_query, 2 * (BQ // BK), BK), jnp.float32),
            pltpu.VMEM((width, tokens), jnp.float32),
            pltpu.VMEM((width, tokens), jnp.float32),
            dma((n_seq, n_query)), dma((n_seq, n_query)),
            dma((n_seq,)), dma((n_seq,)),
            dma((n_head, n_query)), dma((n_head, n_query)),
        ],
        compiler_params=pltpu.CompilerParams(
            collective_id=0, has_side_effects=True, vmem_limit_bytes=44 * 1024 * 1024
        ),
    )(bias, packed, queries[0].T, keys[0].T, values[0].T, coef, gains)
    return out.T[None]


def solution(mesh):
    in_specs = (
        P("head", "seq", None),
        P("head", "seq", None),
        P("head", "seq", None),
        P("head", None, None),
        P(),
        P("head", None),
        P("head", None),
    )
    out_specs = P("head", "seq", None)
    return jax.shard_map(body, mesh=mesh, in_specs=in_specs, out_specs=out_specs, check_vma=False)
```

time: 88 us -> 36.8 us (0.42)
  blocking collectives: 42.7 us -> 0 us
  Pallas kernels: 0 us -> 32.5 us
  between operations: 13.6 us -> 0.08 us
  matrix products: 10.7 us -> 0 us
  starting transfers between devices: 5.3 us -> 0 us
  other arithmetic: 5.54 us -> 0.7 us
  waiting for transfers between devices: 4.46 us -> 0 us
  local copies, waits for them, and re-layouts: 5.17 us -> 3.39 us
    pallas_call x0 -> x2, Pallas kernels: none -> 32.5 us  [the longest x1 31.6 us: body(): pl.pallas_call(functools.partial(kernel, n_seq, n_head, n_query, n_key, n...]
    psum x1 -> x0, blocking collectives: 28.5 us -> none  [body(): lax.psum((square_sparse, square_linear), 'head')]
    all_gather x1 -> x0, blocking collectives: 14.3 us -> none  [body(): lax.all_gather(key_sums, 'seq', axis=0, tiled=True)]
    dot_general x15 -> x0, matrix products: 10.7 us -> none  [the longest x4 2.69 us: attend(): jnp.dot(weights.astype(jnp.bfloat16), values_block, preferred_element_typ...]
    all_to_all x1 -> x0, starting transfers between devices: 5.3 us -> none  [body(): lax.all_to_all(outgoing, 'seq', split_axis=0, concat_axis=2, tiled=True)]
    all_gather x1 -> x0, waiting for transfers between devices: 4.43 us -> none  [body(): lax.all_gather(states, 'seq', axis=0, tiled=True)]
    reshape x8 -> x3, local copies, waits for them, and re-layouts: 3.4 us -> 0.3 us  [the longest x1 0.13 us: body(): coef = jnp.repeat(coef, width, axis=2)]
    reduce_sum x7 -> x2, other arithmetic: 3.1 us -> 0.26 us  [the longest x1 0.15 us: body(): count = jnp.sum(own.reshape(n_query, n_seq, n_key), axis=2)]
  transfers between devices with their start and end apart: 2 -> 0, of which waited for: 1 -> 0; matrix products, arithmetic and copies ran while one was open for 14% -> 0% of each run, Pallas kernels for 0% -> 0%
where the time goes in v1:
time: 36.8 us; the launch traced here: 36.6 us
  Pallas kernels  32.5 us (88%)
  local copies, waits for them, and re-layouts  3.39 us (9%)
  other arithmetic  0.7 us (2%)
    pallas_call x1, Pallas kernels, body(): pl.pallas_call(functools.partial(kernel, n_seq, n_head, n_query, n_key, n...  31.6 us
    unnamed x15, local copies, waits for them, and re-layouts  2.47 us
    pallas_call x1, Pallas kernels, body(): pl.pallas_call(pack, out_shape=jax.ShapeDtypeStruct((n_seq, n_query, 2, w...  0.83 us

profile of v1, /device:TPU:0, one launch (start us, length us, event | category | flops | bytes accessed | tf_op | source)
XLA Modules:
  0.0 36.6 jit_solution(4789852474919329029)
XLA Ops:
  0.0 0.7 %copy-done.5 = f32[1,64]{1,0:T(1,128)S(1)} copy-done((f32[1,64]{1,0:T(1,128)S(1)}, f32[1,64]{1,0:T(1,128)}, u32[]{:S(2)}) %copy-start.5) | copy-done | bytes 280
  0.7 0.0 copy-done.6
  0.7 0.6 %copy-done.4 = s32[16]{0:T(128)S(1)} copy-done((s32[16]{0:T(128)S(1)}, s32[16]{0:T(128)}, u32[]{:S(2)}) %copy-start.4) | copy-done | bytes 88
  1.3 0.1 iota_compare_fusion
  1.4 0.1 select_reduce_fusion
  1.5 0.2 select_reduce_fusion.2
  1.8 0.1 convert_subtract_fusion
  1.9 0.1 reshape.50
  1.9 0.1 reduce_sum.19
  2.1 0.1 fusion
  2.2 0.1 select_n.28.bias_ref
  2.3 0.0 copy-start
  2.3 0.1 copy.18
  2.4 0.1 reshape.51.pick_ref
  2.5 0.1 copy.20
  2.6 0.1 copy.19
  2.7 0.2 broadcast_in_dim.63
  2.9 0.1 reshape.53.coef_ref
  3.0 0.1 copy-done.1
  3.1 0.1 copy-done
  3.2 0.8 %shard_map.73.send = bf16[4,4,2,64,256]{4,3,2,1,0:T(8,128)(2,1)S(1)} custom-call(s32[32]{0:T(128)S(1)} %reshape.51.pick_ref, bf16[64,2048]{1,0:T(8,128)(2,1)S(1)} %bitcast.21, bf16[64,2048]{1,0:T(8,128)(2,1)S(1)} %bitcast.23), custom_call_target="tpu_custom_call" | custom-call | tf_op jit(solution)/shard_map/pallas_call | solution.py:233
  4.1 0.1 copy-done.2
  4.2 31.6 %shard_map.74 = f32[64,2048]{1,0:T(8,128)S(1)} custom-call(f32[32]{0:T(128)S(1)} %select_n.28.bias_ref, bf16[4,4,2,64,256]{4,3,2,1,0:T(8,128)(2,1)S(1)} %shard_map.73.send, bf16[64,2048]{1,0:T(8,128)(2,1)S(1)} %bitcast.25, bf16[64,2048]{1,0:T(8,128)(2,1)S(1)} %bitcast.22, bf16[64,2048]{1,0:T(8,128)(2,1)S(1)} %bitcast.24, ...), custom_call_target="tpu_custom_call" | custom-call | tf_op jit(solution)/shard_map/pallas_call | solution.py:242
  35.8 0.8 %copy.22 = f32[1,2048,64]{1,2,0:T(8,128)} copy(f32[1,2048,64]{1,2,0:T(8,128)S(1)} %bitcast.20) | data formatting | bytes 1048576
  (11 shorter events, 0.0 us)
Async XLA Ops:
  0.0 1.4 %copy-start.3 = (s32[1,16,64]{2,1,0:T(8,128)S(1)}, s32[1,16,64]{2,1,0:T(8,128)}, u32[]{:S(2)}) copy-start(s32[1,16,64]{2,1,0:T(8,128)} %param.10) | copy-start | bytes 12292
  0.0 0.7 %copy-start.5 = (f32[1,64]{1,0:T(1,128)S(1)}, f32[1,64]{1,0:T(1,128)}, u32[]{:S(2)}) copy-start(f32[1,64]{1,0:T(1,128)} %param.13) | copy-start | bytes 772
  0.0 0.7 %copy-start.6 = (f32[1,64]{1,0:T(1,128)S(1)}, f32[1,64]{1,0:T(1,128)}, u32[]{:S(2)}) copy-start(f32[1,64]{1,0:T(1,128)} %param.12) | copy-start | bytes 772
  0.7 0.7 %copy-start.4 = (s32[16]{0:T(128)S(1)}, s32[16]{0:T(128)}, u32[]{:S(2)}) copy-start(s32[16]{0:T(128)} %param.11) | copy-start | bytes 196
  2.2 1.0 %copy-start.1 = (bf16[1,2048,64]{1,2,0:T(8,128)(2,1)S(1)}, bf16[1,2048,64]{1,2,0:T(8,128)(2,1)}, u32[]{:S(2)}) copy-start(bf16[1,2048,64]{1,2,0:T(8,128)(2,1)} %param.9) | copy-start | bytes 786436
  2.3 1.0 %copy-start = (bf16[1,2048,64]{1,2,0:T(8,128)(2,1)S(1)}, bf16[1,2048,64]{1,2,0:T(8,128)(2,1)}, u32[]{:S(2)}) copy-start(bf16[1,2048,64]{1,2,0:T(8,128)(2,1)} %param.8) | copy-start | bytes 786436
  3.2 0.9 %copy-start.2 = (bf16[1,2048,64]{1,2,0:T(8,128)(2,1)S(1)}, bf16[1,2048,64]{1,2,0:T(8,128)(2,1)}, u32[]{:S(2)}) copy-start(bf16[1,2048,64]{1,2,0:T(8,128)(2,1)} %param.7) | copy-start | bytes 786436

commit v2 on v1

--- a/solution.py
+++ b/solution.py
@@ -34,7 +34,7 @@
 
 def kernel(
     n_seq, n_head, n_query, n_key, features,
-    bias_ref, send, q_ref, k_ref, v_ref, coef_ref, gain_ref, out_ref,
+    bias_ref, open_ref, send, q_ref, k_ref, v_ref, gain_sparse_ref, gain_linear_ref, out_ref,
     recv, usend, urecv, states, scores, sq, linear_ref, sparse_ref,
     kv_send_sem, kv_recv_sem, u_send_sem, u_recv_sem, sq_send_sem, sq_recv_sem,
 ):
@@ -80,13 +80,6 @@
     @pl.loop(1, n_head)
     def _(o):
         pl.semaphore_signal(barrier, inc=1, device_id={"head": head_peer(o)}, device_id_type=MESH)
-
-    pl.semaphore_wait(barrier, n_seq + n_head - 2)
-    for b in range(n_query):
-
-        @pl.loop(1, n_seq)
-        def _(o):
-            kv_copy(peer(o), me, b).start()
 
     ones = jnp.ones((16, BK), jnp.bfloat16)
     for j in range(n_key):
@@ -101,82 +94,104 @@
         state += lax.dot_general(wide, low, dims, preferred_element_type=jnp.float32)
         states[j] = state[:rows]
 
+    low_half = lax.broadcasted_iota(jnp.int32, (1, 2 * width), 1) < width
+
     def combine(dev, target, place):
         for p in range(pairs):
             total = jnp.zeros((rows, 2 * width), jnp.float32)
+            at = dev * n_query + 2 * p
             for j in range(n_key):
-                total += states[j] * coef_ref[dev * pairs + p, j : j + 1, :]
+                total += states[j] * jnp.where(low_half, open_ref[at, j], open_ref[at + 1, j])
             target[place, p] = total
 
     @pl.loop(1, n_seq)
     def _(o):
         combine(peer(o), usend, peer(o))
+
+    pl.semaphore_wait(barrier, n_seq + n_head - 2)
+
+    def send_blocks(b):
+        @pl.loop(1, n_seq)
+        def _(o):
+            kv_copy(peer(o), me, b).start()
+
+    send_blocks(0)
+
+    @pl.loop(1, n_seq)
+    def _(o):
         u_copy(peer(o), me).start()
+
+    for b in range(1, n_query):
+        send_blocks(b)
 
     combine(me, urecv, me)
     recv[me] = send[me]
 
-    @pl.loop(1, n_seq)
-    def _(o):
-        u_copy(peer(o), peer(o)).wait_recv()
+    def span(b):
+        return pl.ds(pl.multiple_of(b * BQ, BQ), BQ)
+
+    def attend(b):
+        scaled = (q_ref[:, span(b)].astype(jnp.float32) * width ** (-0.5)).astype(jnp.bfloat16)
+
+        @pl.loop(1, n_seq)
+        def _(o):
+            kv_copy(peer(o), peer(o), b).wait_recv()
+
+        top = jnp.full((1, BQ), NEGATIVE, jnp.float32)
+        for src in range(n_seq):
+            part = lax.dot_general(
+                recv[src, b, 0], scaled, (((0,), (0,)), ((), ())),
+                preferred_element_type=jnp.float32,
+            )
+            for s in range(SLOTS):
+                one = part[s * BK : (s + 1) * BK] + bias_ref[b, src * SLOTS + s]
+                scores[src, s * BK : (s + 1) * BK] = one
+                top = jnp.maximum(top, jnp.max(one, axis=0, keepdims=True))
+        total = jnp.zeros((1, BQ), jnp.float32)
+        acc = jnp.zeros((width, BQ), jnp.float32)
+        for src in range(n_seq):
+            weights = jnp.exp(scores[src] - top)
+            total += jnp.sum(weights, axis=0, keepdims=True)
+            acc += jnp.dot(
+                recv[src, b, 1], weights.astype(jnp.bfloat16),
+                preferred_element_type=jnp.float32,
+            )
+        sparse_ref[:, span(b)] = acc * (1.0 / total)
+
+    def attend_linear():
+        for p in range(pairs):
+            state = urecv[0, p]
+            for src in range(1, n_seq):
+                state += urecv[src, p]
+            for half in range(2):
+                b = p * 2 + half
+                mine = jnp.dot(
+                    state[:, half * width : (half + 1) * width],
+                    phi(q_ref[:, b * BQ : (b + 1) * BQ].astype(jnp.float32)),
+                    preferred_element_type=jnp.float32, precision=lax.Precision.HIGH,
+                )
+                linear_ref[:, b * BQ : (b + 1) * BQ] = mine[:width] * (1.0 / mine[width : width + 1])
 
     def sums(x):
         total = jnp.sum(x * x, axis=0, keepdims=True)
         return [total[:, i * BK : (i + 1) * BK] for i in range(BQ // BK)]
 
-    @pl.loop(0, pairs)
-    def _(p):
-        state = urecv[0, p]
-        for src in range(1, n_seq):
-            state += urecv[src, p]
-        for half in range(2):
-            b = p * 2 + half
-            here = pl.ds(pl.multiple_of(b * BQ, BQ), BQ)
-            query = q_ref[:, here].astype(jnp.float32)
-            mine = jnp.dot(
-                state[:, half * width : (half + 1) * width], phi(query),
-                preferred_element_type=jnp.float32, precision=lax.Precision.HIGH,
-            )
-            linear = mine[:width] / mine[width : width + 1]
-            linear_ref[:, here] = linear
-            scaled = (query * width ** (-0.5)).astype(jnp.bfloat16)
-
-            @pl.loop(1, n_seq)
-            def _(o):
-                kv_copy(peer(o), peer(o), b).wait_recv()
-
-            top = jnp.full((1, BQ), NEGATIVE, jnp.float32)
-            for src in range(n_seq):
-                part = lax.dot_general(
-                    recv[src, b, 0], scaled, (((0,), (0,)), ((), ())),
-                    preferred_element_type=jnp.float32,
-                )
-                for s in range(SLOTS):
-                    one = part[s * BK : (s + 1) * BK] + bias_ref[(b * n_seq + src) * SLOTS + s]
-                    scores[src, s * BK : (s + 1) * BK] = one
-                    top = jnp.maximum(top, jnp.max(one, axis=0, keepdims=True))
-            total = jnp.zeros((1, BQ), jnp.float32)
-            acc = jnp.zeros((width, BQ), jnp.float32)
-            for src in range(n_seq):
-                weights = jnp.exp(scores[src] - top)
-                total += jnp.sum(weights, axis=0, keepdims=True)
-                acc += jnp.dot(
-                    recv[src, b, 1], weights.astype(jnp.bfloat16),
-                    preferred_element_type=jnp.float32,
-                )
-            sparse = acc / total
-            sparse_ref[:, here] = sparse
-            sq[head, b] = jnp.concatenate(sums(sparse) + sums(linear), axis=0)
-
-            @pl.loop(1, n_head)
-            def _(o):
-                sq_copy(head_peer(o), head, b).start()
-
-    gain_sparse = gain_ref[:, 0:1]
-    gain_linear = gain_ref[:, 1:2]
-
-    @pl.loop(0, n_query)
-    def _(b):
+    def share(b):
+        sq[head, b] = jnp.concatenate(
+            sums(sparse_ref[:, span(b)]) + sums(linear_ref[:, span(b)]), axis=0
+        )
+
+        @pl.loop(1, n_head)
+        def _(o):
+            sq_copy(head_peer(o), head, b).start()
+
+    diagonal = lax.broadcasted_iota(jnp.int32, (width, width), 0) == lax.broadcasted_iota(
+        jnp.int32, (width, width), 1
+    )
+    gain_sparse = jnp.sum(jnp.where(diagonal, gain_sparse_ref[...], 0.0), axis=1, keepdims=True)
+    gain_linear = jnp.sum(jnp.where(diagonal, gain_linear_ref[...], 0.0), axis=1, keepdims=True)
+
+    def finish(b):
         @pl.loop(1, n_head)
         def _(o):
             sq_copy(head_peer(o), head_peer(o), b).wait_recv()
@@ -191,6 +206,23 @@
             first = sparse_ref[:, here] * scale[i : i + 1] * gain_sparse
             second = linear_ref[:, here] * scale[parts + i : parts + i + 1] * gain_linear
             out_ref[:, here] = first + second
+
+    attend(0)
+
+    @pl.loop(1, n_seq)
+    def _(o):
+        u_copy(peer(o), peer(o)).wait_recv()
+
+    attend_linear()
+    share(0)
+
+    @pl.loop(1, n_query)
+    def _(b):
+        attend(b)
+        share(b)
+        finish(b - 1)
+
+    finish(n_query - 1)
 
     @pl.loop(1, n_seq)
     def _(o):
@@ -221,11 +253,8 @@
     pick = jnp.stack([jnp.minimum(first, n_key - 1), last], axis=1).reshape(-1)
     count = jnp.sum(own.reshape(n_query, n_seq, n_key), axis=2)
     slot = jnp.arange(SLOTS, dtype=jnp.int32)
-    bias = jnp.where(slot < count[:, :, None], 0.0, NEGATIVE).astype(jnp.float32).reshape(-1)
-    open_blocks = 1.0 - local.astype(jnp.float32)
-    coef = open_blocks.reshape(n_seq * pairs, 2, n_key).swapaxes(1, 2)
-    coef = jnp.repeat(coef, width, axis=2)
-    gains = jnp.concatenate([sparse_gain, linear_gain], axis=0).T
+    bias = jnp.where(slot < count[:, :, None], 0.0, NEGATIVE).astype(jnp.float32).reshape(n_query, -1)
+    opened = 1.0 - local.astype(jnp.float32)
     rows = width + 8
     vmem = pl.BlockSpec(memory_space=pltpu.VMEM)
     smem = pl.BlockSpec(memory_space=pltpu.SMEM)
@@ -244,7 +273,7 @@
             kernel, n_seq, n_head, n_query, n_key, n_head * queries.shape[0] * width
         ),
         out_shape=jax.ShapeDtypeStruct((width, tokens), jnp.float32),
-        in_specs=[smem] + [vmem] * 6,
+        in_specs=[smem, smem] + [vmem] * 6,
         out_specs=vmem,
         scratch_shapes=[
             pltpu.VMEM((n_seq, n_query, 2, width, SLOTS * BK), jnp.bfloat16),
@@ -262,7 +291,9 @@
         compiler_params=pltpu.CompilerParams(
             collective_id=0, has_side_effects=True, vmem_limit_bytes=44 * 1024 * 1024
         ),
-    )(bias, packed, queries[0].T, keys[0].T, values[0].T, coef, gains)
+    )(
+        bias, opened, packed, queries[0].T, keys[0].T, values[0].T, sparse_gain, linear_gain
+    )
     return out.T[None]
 
 

time: 36.8 us -> 33.8 us (0.918)
  Pallas kernels: 32.5 us -> 28.8 us
  local copies, waits for them, and re-layouts: 3.39 us -> 4.1 us
    pallas_call x1, Pallas kernels: 31.6 us -> 28 us  [body(): pl.pallas_call(functools.partial(kernel, n_seq, n_head, n_query, n_key, n...]
    unnamed x15 -> x17, local copies, waits for them, and re-layouts: 2.47 us -> 3.55 us
where the time goes in v2:
time: 33.8 us; the launch traced here: 33.6 us
  Pallas kernels  28.8 us (85%)
  local copies, waits for them, and re-layouts  4.1 us (12%)
  other arithmetic  0.63 us (2%)
    pallas_call x1, Pallas kernels, body(): pl.pallas_call(functools.partial(kernel, n_seq, n_head, n_query, n_key, n...  28 us
    unnamed x17, local copies, waits for them, and re-layouts  3.55 us
    pallas_call x1, Pallas kernels, body(): pl.pallas_call(pack, out_shape=jax.ShapeDtypeStruct((n_seq, n_query, 2, w...  0.84 us

profile of v2, /device:TPU:0, one launch (start us, length us, event | category | flops | bytes accessed | tf_op | source)
XLA Modules:
  0.0 33.6 jit_solution(17286026590373629105)
XLA Ops:
  0.0 0.0 copy-start.6
  0.0 0.7 %copy-done.7 = s32[16]{0:T(128)S(1)} copy-done((s32[16]{0:T(128)S(1)}, s32[16]{0:T(128)}, u32[]{:S(2)}) %copy-start.7) | copy-done | bytes 88
  0.7 0.1 iota_compare_fusion
  0.7 0.1 lt.27
  0.8 0.0 copy-done.6
  0.8 0.1 select_reduce_fusion
  1.0 0.2 select_reduce_fusion.2
  1.2 0.1 convert_subtract_fusion.open_ref
  1.3 0.1 reshape.40
  1.4 0.1 reduce_sum.19
  1.5 0.1 copy.15
  1.6 0.1 copy.16
  1.7 0.1 copy.17
  1.8 0.1 reshape.41.pick_ref
  1.9 0.0 copy-start
  1.9 0.9 %copy-done = bf16[1,2048,64]{1,2,0:T(8,128)(2,1)S(1)} copy-done((bf16[1,2048,64]{1,2,0:T(8,128)(2,1)S(1)}, bf16[1,2048,64]{1,2,0:T(8,128)(2,1)}, u32[]{:S(2)}) %copy-start) | copy-done | bytes 262168
  2.8 0.9 %copy-done.2 = bf16[1,2048,64]{1,2,0:T(8,128)(2,1)S(1)} copy-done((bf16[1,2048,64]{1,2,0:T(8,128)(2,1)S(1)}, bf16[1,2048,64]{1,2,0:T(8,128)(2,1)}, u32[]{:S(2)}) %copy-start.2) | copy-done | bytes 262168
  3.8 0.8 %shard_map.73.send = bf16[4,4,2,64,256]{4,3,2,1,0:T(8,128)(2,1)S(1)} custom-call(s32[32]{0:T(128)S(1)} %reshape.41.pick_ref, bf16[64,2048]{1,0:T(8,128)(2,1)S(1)} %bitcast.18, bf16[64,2048]{1,0:T(8,128)(2,1)S(1)} %bitcast.20), custom_call_target="tpu_custom_call" | custom-call | tf_op jit(solution)/shard_map/pallas_call | solution.py:262
  4.6 0.1 copy-done.1
  4.7 0.1 copy-done.3
  4.8 0.0 copy-done.4
  4.8 0.0 copy-done.5
  4.8 28.0 %shard_map.74 = f32[64,2048]{1,0:T(8,128)S(1)} custom-call(f32[4,8]{1,0:T(4,128)S(1)} %compare_select_fusion.bias_ref, f32[16,16]{1,0:T(8,128)S(1)} %convert_subtract_fusion.open_ref, bf16[4,4,2,64,256]{4,3,2,1,0:T(8,128)(2,1)S(1)} %shard_map.73.send, bf16[64,2048]{1,0:T(8,128)(2,1)S(1)} %bitcast.22, bf16[64,2048]{1,0:T(8,128)(2,1)S(1)} %bitcast.19, ...), custom_call_target="tpu_custom_call" | custom-call | tf_op jit(solution)/shard_map/pallas_call | solution.py:271
  32.8 0.8 %copy.19 = f32[1,2048,64]{1,2,0:T(8,128)} copy(f32[1,2048,64]{1,2,0:T(8,128)S(1)} %bitcast.17) | data formatting | bytes 1048576
  (12 shorter events, 0.1 us)
Async XLA Ops:
  0.0 0.8 %copy-start.6 = (s32[1,16,64]{2,1,0:T(8,128)S(1)}, s32[1,16,64]{2,1,0:T(8,128)}, u32[]{:S(2)}) copy-start(s32[1,16,64]{2,1,0:T(8,128)} %param.10) | copy-start | bytes 12292
  0.0 0.7 %copy-start.7 = (s32[16]{0:T(128)S(1)}, s32[16]{0:T(128)}, u32[]{:S(2)}) copy-start(s32[16]{0:T(128)} %param.11) | copy-start | bytes 196
  1.9 1.0 %copy-start = (bf16[1,2048,64]{1,2,0:T(8,128)(2,1)S(1)}, bf16[1,2048,64]{1,2,0:T(8,128)(2,1)}, u32[]{:S(2)}) copy-start(bf16[1,2048,64]{1,2,0:T(8,128)(2,1)} %param.8) | copy-start | bytes 786436
  2.8 0.9 %copy-start.2 = (bf16[1,2048,64]{1,2,0:T(8,128)(2,1)S(1)}, bf16[1,2048,64]{1,2,0:T(8,128)(2,1)}, u32[]{:S(2)}) copy-start(bf16[1,2048,64]{1,2,0:T(8,128)(2,1)} %param.9) | copy-start | bytes 786436
  3.8 0.9 %copy-start.1 = (bf16[1,2048,64]{1,2,0:T(8,128)(2,1)S(1)}, bf16[1,2048,64]{1,2,0:T(8,128)(2,1)}, u32[]{:S(2)}) copy-start(bf16[1,2048,64]{1,2,0:T(8,128)(2,1)} %param.8) | copy-start | bytes 786436
  3.8 1.0 %copy-start.3 = (bf16[1,2048,64]{1,2,0:T(8,128)(2,1)S(1)}, bf16[1,2048,64]{1,2,0:T(8,128)(2,1)}, u32[]{:S(2)}) copy-start(bf16[1,2048,64]{1,2,0:T(8,128)(2,1)} %param.7) | copy-start | bytes 786436
  3.8 1.0 %copy-start.4 = (f32[1,64]{1,0:T(1,128)S(1)}, f32[1,64]{1,0:T(1,128)}, u32[]{:S(2)}) copy-start(f32[1,64]{1,0:T(1,128)} %gain_sparse_ref.1) | copy-start | bytes 772
  3.8 1.0 %copy-start.5 = (f32[1,64]{1,0:T(1,128)S(1)}, f32[1,64]{1,0:T(1,128)}, u32[]{:S(2)}) copy-start(f32[1,64]{1,0:T(1,128)} %gain_linear_ref.1) | copy-start | bytes 772

commit v3 on v2

--- a/solution.py
+++ b/solution.py
@@ -19,14 +19,14 @@
     return jnp.where(x > 0, x + 1.0, jnp.exp(jnp.minimum(x, 0.0)))
 
 
-def pack(pick_ref, k_ref, v_ref, out_ref):
+def pack(first_ref, last_ref, k_ref, v_ref, out_ref):
     n_seq, n_query = out_ref.shape[:2]
 
     @pl.loop(0, n_seq)
     def _(dev):
         for b in range(n_query):
-            for s in range(SLOTS):
-                block = pick_ref[(dev * n_query + b) * SLOTS + s]
+            for s, pick_ref in enumerate((first_ref, last_ref)):
+                block = pick_ref[dev * n_query + b]
                 columns = pl.ds(pl.multiple_of(block * BK, BK), BK)
                 out_ref[dev, b, 0, :, s * BK : (s + 1) * BK] = k_ref[:, columns]
                 out_ref[dev, b, 1, :, s * BK : (s + 1) * BK] = v_ref[:, columns]
@@ -250,7 +250,7 @@
     column = jnp.arange(n_key, dtype=jnp.int32)[None, :]
     first = jnp.min(jnp.where(local > 0, column, n_key), axis=1)
     last = jnp.max(jnp.where(local > 0, column, 0), axis=1)
-    pick = jnp.stack([jnp.minimum(first, n_key - 1), last], axis=1).reshape(-1)
+    first = jnp.minimum(first, n_key - 1)
     count = jnp.sum(own.reshape(n_query, n_seq, n_key), axis=2)
     slot = jnp.arange(SLOTS, dtype=jnp.int32)
     bias = jnp.where(slot < count[:, :, None], 0.0, NEGATIVE).astype(jnp.float32).reshape(n_query, -1)
@@ -264,10 +264,10 @@
         out_shape=jax.ShapeDtypeStruct(
             (n_seq, n_query, 2, width, SLOTS * BK), jnp.bfloat16
         ),
-        in_specs=[smem, vmem, vmem],
+        in_specs=[smem, smem, vmem, vmem],
         out_specs=vmem,
         compiler_params=pltpu.CompilerParams(vmem_limit_bytes=24 * 1024 * 1024),
-    )(pick, keys[0].T, values[0].T)
+    )(first, last, keys[0].T, values[0].T)
     out = pl.pallas_call(
         functools.partial(
             kernel, n_seq, n_head, n_query, n_key, n_head * queries.shape[0] * width

time: 33.8 us -> 33.6 us (level)
  no operation moved by 1% of the time
where the time goes in v3:
time: 33.6 us; the launch traced here: 33.4 us
  Pallas kernels  28.8 us (86%)
  local copies, waits for them, and re-layouts  3.93 us (12%)
  other arithmetic  0.62 us (2%)
    pallas_call x1, Pallas kernels, body(): pl.pallas_call(functools.partial(kernel, n_seq, n_head, n_query, n_key, n...  28 us
    unnamed x17, local copies, waits for them, and re-layouts  3.56 us
    pallas_call x1, Pallas kernels, body(): pl.pallas_call(pack, out_shape=jax.ShapeDtypeStruct((n_seq, n_query, 2, w...  0.84 us

profile of v3, /device:TPU:0, one launch (start us, length us, event | category | flops | bytes accessed | tf_op | source)
XLA Modules:
  0.0 33.4 jit_solution(12536380844601506670)
XLA Ops:
  0.0 0.0 copy-start.7
  0.0 0.7 %copy-done.7 = s32[16]{0:T(128)S(1)} copy-done((s32[16]{0:T(128)S(1)}, s32[16]{0:T(128)}, u32[]{:S(2)}) %copy-start.7) | copy-done | bytes 88
  0.7 0.1 iota_compare_fusion
  0.7 0.1 lt.27
  0.8 0.0 copy-done.6
  0.8 0.1 select_reduce_fusion
  1.0 0.2 select_reduce_fusion.1
  1.2 0.1 convert_subtract_fusion.open_ref
  1.3 0.1 reshape.28
  1.3 0.1 reduce_sum.19
  1.5 0.1 copy.12
  1.6 0.1 copy.13
  1.7 0.0 copy-start
  1.7 1.0 %copy-done = bf16[1,2048,64]{1,2,0:T(8,128)(2,1)S(1)} copy-done((bf16[1,2048,64]{1,2,0:T(8,128)(2,1)S(1)}, bf16[1,2048,64]{1,2,0:T(8,128)(2,1)}, u32[]{:S(2)}) %copy-start) | copy-done | bytes 262168
  2.6 0.0 copy-start.2
  2.6 0.9 %copy-done.2 = bf16[1,2048,64]{1,2,0:T(8,128)(2,1)S(1)} copy-done((bf16[1,2048,64]{1,2,0:T(8,128)(2,1)S(1)}, bf16[1,2048,64]{1,2,0:T(8,128)(2,1)}, u32[]{:S(2)}) %copy-start.2) | copy-done | bytes 262168
  3.6 0.0 copy-start.1
  3.6 0.8 %shard_map.73.send = bf16[4,4,2,64,256]{4,3,2,1,0:T(8,128)(2,1)S(1)} custom-call(s32[16]{0:T(128)S(1)} %broadcast_minimum_fusion.first_ref, s32[16]{0:T(128)S(1)} %get-tuple-element.5.last_ref, bf16[64,2048]{1,0:T(8,128)(2,1)S(1)} %bitcast.15, bf16[64,2048]{1,0:T(8,128)(2,1)S(1)} %bitcast.17), custom_call_target="tpu_custom_call" | custom-call | tf_op jit(solution)/shard_map/pallas_call | solution.py:262
  4.5 0.1 copy-done.1
  4.5 0.1 copy-done.3
  4.6 0.0 copy-done.4
  4.6 0.0 copy-done.5
  4.6 28.0 %shard_map.74 = f32[64,2048]{1,0:T(8,128)S(1)} custom-call(f32[4,8]{1,0:T(4,128)S(1)} %compare_select_fusion.bias_ref, f32[16,16]{1,0:T(8,128)S(1)} %convert_subtract_fusion.open_ref, bf16[4,4,2,64,256]{4,3,2,1,0:T(8,128)(2,1)S(1)} %shard_map.73.send, bf16[64,2048]{1,0:T(8,128)(2,1)S(1)} %bitcast.19, bf16[64,2048]{1,0:T(8,128)(2,1)S(1)} %bitcast.16, ...), custom_call_target="tpu_custom_call" | custom-call | tf_op jit(solution)/shard_map/pallas_call | solution.py:271
  32.6 0.8 %copy.15 = f32[1,2048,64]{1,2,0:T(8,128)} copy(f32[1,2048,64]{1,2,0:T(8,128)S(1)} %bitcast.14) | data formatting | bytes 1048576
  (9 shorter events, 0.0 us)
Async XLA Ops:
  0.0 0.8 %copy-start.6 = (s32[1,16,64]{2,1,0:T(8,128)S(1)}, s32[1,16,64]{2,1,0:T(8,128)}, u32[]{:S(2)}) copy-start(s32[1,16,64]{2,1,0:T(8,128)} %param.10) | copy-start | bytes 12292
  0.0 0.7 %copy-start.7 = (s32[16]{0:T(128)S(1)}, s32[16]{0:T(128)}, u32[]{:S(2)}) copy-start(s32[16]{0:T(128)} %param.11) | copy-start | bytes 196
  1.7 1.0 %copy-start = (bf16[1,2048,64]{1,2,0:T(8,128)(2,1)S(1)}, bf16[1,2048,64]{1,2,0:T(8,128)(2,1)}, u32[]{:S(2)}) copy-start(bf16[1,2048,64]{1,2,0:T(8,128)(2,1)} %param.8) | copy-start | bytes 786436
  2.6 0.9 %copy-start.2 = (bf16[1,2048,64]{1,2,0:T(8,128)(2,1)S(1)}, bf16[1,2048,64]{1,2,0:T(8,128)(2,1)}, u32[]{:S(2)}) copy-start(bf16[1,2048,64]{1,2,0:T(8,128)(2,1)} %param.9) | copy-start | bytes 786436
  3.6 0.9 %copy-start.1 = (bf16[1,2048,64]{1,2,0:T(8,128)(2,1)S(1)}, bf16[1,2048,64]{1,2,0:T(8,128)(2,1)}, u32[]{:S(2)}) copy-start(bf16[1,2048,64]{1,2,0:T(8,128)(2,1)} %param.8) | copy-start | bytes 786436
  3.6 1.0 %copy-start.3 = (bf16[1,2048,64]{1,2,0:T(8,128)(2,1)S(1)}, bf16[1,2048,64]{1,2,0:T(8,128)(2,1)}, u32[]{:S(2)}) copy-start(bf16[1,2048,64]{1,2,0:T(8,128)(2,1)} %param.7) | copy-start | bytes 786436
  3.6 1.0 %copy-start.4 = (f32[1,64]{1,0:T(1,128)S(1)}, f32[1,64]{1,0:T(1,128)}, u32[]{:S(2)}) copy-start(f32[1,64]{1,0:T(1,128)} %gain_sparse_ref.1) | copy-start | bytes 772
  3.6 1.0 %copy-start.5 = (f32[1,64]{1,0:T(1,128)S(1)}, f32[1,64]{1,0:T(1,128)}, u32[]{:S(2)}) copy-start(f32[1,64]{1,0:T(1,128)} %gain_linear_ref.1) | copy-start | bytes 772
